TPU v7x, 256 devices: a whole 4x4x8 slice. The times are simulated.
256 devices in a mesh: shot: 8 (over y, core), band: 32 (over x, z).
Axes of the slice: x: 4, y: 4, z: 8, core: 2. Of those that a mesh axis runs over, the one named last changes fastest.
Arguments:
- sensitivity: bfloat16 [16384, 128, 128], P(('shot', 'band')), may hold values from -0.0625 to 0.0625
- bundle_of: int32 [16384], P(('shot', 'band')), may hold values from 0 to 31
- cellblock_of: int32 [16384], P(('shot', 'band')), may hold values from 0 to 15
- state: float32 [65536, 128], P('band'), may hold values from -6 to 6
- prior_velocity: float32 [65536, 128], P('band'), may hold values from -6 to 6
- observed: float32 [256, 128], P(('shot', 'band')), may hold values from -6 to 6
- pick_weight: float32 [256, 128], P(('shot', 'band')), may hold values from 0.3 to 3
Outputs:
- new_state: float32 [65536, 128], P('band')
- weighted_residual: float32 [256, 128, 128], P(('shot', 'band'))
Inputs may be any that keep to these rules, and one draw needn't show every extreme that they name: bundle_of names a bundle of the block's own source group. cellblock_of names a cell block of the block's own depth band.
All inputs are finite; a program needn't handle non-finite values.
Results may differ from a plain program's by a relative error of at most 0.0059.
Values may be sent and summed in bfloat16 or wider, within the bound.
A program may use at most 64 MiB of HBM per device.

v0:
```python
import jax
import jax.numpy as jnp
from jax import lax
from jax.sharding import PartitionSpec as P

CBLK = 128


def block_products(sensitivity, cellblock_of, probe):
    columns = probe.reshape(-1, CBLK, probe.shape[1])[cellblock_of]
    return jnp.einsum("krc,kce->kre", sensitivity, columns, preferred_element_type=jnp.float32)


def adjoint_part(sensitivity, bundle_of, cellblock_of, resid_all, cell_blocks):
    rows = resid_all[bundle_of]
    contrib = jnp.einsum("krc,kre->kce", sensitivity, rows, preferred_element_type=jnp.float32)
    summed = jax.ops.segment_sum(contrib, cellblock_of, num_segments=cell_blocks)
    return summed.reshape(cell_blocks * CBLK, rows.shape[2])


def per_device(sensitivity, bundle_of, cellblock_of, state, prior_velocity, observed, pick_weight):
    nband = lax.axis_size("band")
    owned = observed.shape[0]
    bundles = owned * nband
    cell_blocks = state.shape[0] // CBLK

    def residual_pass(probe):
        prod = block_products(sensitivity, cellblock_of, probe)
        partial_value = jax.ops.segment_sum(prod, bundle_of, num_segments=bundles)
        pred = lax.psum_scatter(partial_value, "band", scatter_dimension=0, tiled=True)
        resid = pick_weight[:, :, None] * (pred - observed[:, :, None])
        resid_all = lax.all_gather(resid.astype(jnp.bfloat16), "band", axis=0, tiled=True)
        return (resid, adjoint_part(sensitivity, bundle_of, cellblock_of, resid_all, cell_blocks))

    probe1 = (state + 0.5 * prior_velocity).astype(jnp.bfloat16)
    res1, part1 = residual_pass(probe1)

    def summed_grad(part):
        return lax.psum(part, "shot")

    grad1 = summed_grad(part1)
    middle = state + 0.5 * (prior_velocity - 0.5 * grad1)
    probe2 = (middle + 0.5 * prior_velocity).astype(jnp.bfloat16)
    res2, part2 = residual_pass(probe2)
    grad2 = summed_grad(part2)
    new_state = state + 0.5 * (prior_velocity - 0.25 * (grad1 + grad2))
    return (new_state, res2)


def solution(mesh):
    in_specs = (
        P(("shot", "band"), None, None),
        P(("shot", "band")),
        P(("shot", "band")),
        P("band", None),
        P("band", None),
        P(("shot", "band"), None),
        P(("shot", "band"), None),
    )
    out_specs = (P("band", None), P(("shot", "band"), None, None))
    return jax.shard_map(
        per_device, mesh=mesh, in_specs=in_specs, out_specs=out_specs, check_vma=False
    )
```

profile of v0, /device:TPU:2, one launch (start us, length us, event | category | flops | bytes accessed | tf_op | source)
XLA Modules:
  0.0 845.8 jit_solution(9297075635177994917)
XLA Ops:
  9.7 2.2 gather_fusion
  11.8 5.2 convolution_bitcast_fusion.3
  17.0 5.6 copy.28
  24.2 13.5 %scatter_fusion = f32[32,128,128]{2,1,0:T(8,128)} fusion(f32[32,128,128]{2,1,0:T(8,128)} %broadcast.21.clone, s32[64]{0:T(128)S(1)} %copy-done.3, f32[64,128,128]{2,1,0:T(8,128)} %copy.28), kind=kCustom, calls=%fused_computation.4 | custom fusion | flops 1048576 | bytes 12583168 | tf_op jit(solution)/shard_map/scatter-add | solution.py:29
  37.8 218.6 %reduce-scatter.3.cloned.1.call-done = f32[1,128,128]{2,1,0:T(8,128)} async-done(((f32[32,128,128]{2,1,0:T(8,128)}), f32[1,128,128]{2,1,0:T(8,128)}) %reduce-scatter.3.cloned.1.call-update) | async-done | bytes 65552 | tf_op jit(solution)/shard_map/reduce_scatter | solution.py:30
  258.0 76.1 %all-gather.3.cloned.1.call-done = bf16[32,128,128]{2,1,0:T(8,128)(2,1)} async-done(((bf16[1,128,128]{2,1,0:T(8,128)(2,1)}), bf16[32,128,128]{2,1,0:T(8,128)(2,1)}) %all-gather.3.cloned.1.call-update) | async-done | bytes 1048592 | tf_op jit(solution)/shard_map/all_gather | solution.py:32
  334.1 3.4 gather_fusion.1
  337.5 4.4 convolution_bitcast_fusion.2
  341.9 5.6 copy.30
  347.6 8.8 %scatter_fusion.1 = f32[16,128,128]{2,1,0:T(8,128)S(1)} fusion(f32[16,128,128]{2,1,0:T(8,128)S(1)} %broadcast.20.clone, s32[64]{0:T(128)S(1)} %copy-done.6, f32[64,128,128]{2,1,0:T(8,128)} %copy.30), kind=kCustom, calls=%fused_computation.5 | custom fusion | flops 1048576 | bytes 12583168 | tf_op jit(solution)/shard_map/scatter-add | solution.py:17
  357.5 66.3 %all-reduce.3.cloned.1.call-done = f32[2048,128]{1,0:T(8,128)} async-done(((f32[2048,128]{1,0:T(8,128)}), f32[2048,128]{1,0:T(8,128)}) %all-reduce.3.cloned.1.call-update) | async-done | bytes 1048592 | tf_op jit(solution)/shard_map/psum | solution.py:39
  423.8 2.1 add_convert_fusion
  425.9 2.2 gather_fusion.2
  428.0 5.2 convolution_bitcast_fusion.1
  433.2 5.6 copy.32
  440.4 13.5 %scatter_fusion.2 = f32[32,128,128]{2,1,0:T(8,128)} fusion(f32[32,128,128]{2,1,0:T(8,128)} %broadcast.21, s32[64]{0:T(128)S(1)} %copy-done.3, f32[64,128,128]{2,1,0:T(8,128)} %copy.32), kind=kCustom, calls=%fused_computation.6 | custom fusion | flops 1048576 | bytes 12583168 | tf_op jit(solution)/shard_map/scatter-add | solution.py:29
  454.0 214.7 %reduce-scatter.5.cloned.1.call-done = f32[1,128,128]{2,1,0:T(8,128)} async-done(((f32[32,128,128]{2,1,0:T(8,128)}), f32[1,128,128]{2,1,0:T(8,128)}) %reduce-scatter.5.cloned.1.call-update) | async-done | bytes 65552 | tf_op jit(solution)/shard_map/reduce_scatter | solution.py:30
  670.5 75.5 %all-gather.5.cloned.1.call-done = bf16[32,128,128]{2,1,0:T(8,128)(2,1)} async-done(((bf16[1,128,128]{2,1,0:T(8,128)(2,1)}), bf16[32,128,128]{2,1,0:T(8,128)(2,1)}) %all-gather.5.cloned.1.call-update) | async-done | bytes 1048592 | tf_op jit(solution)/shard_map/all_gather | solution.py:32
  746.0 3.4 gather_fusion.3
  749.4 4.4 convolution_bitcast_fusion
  753.8 5.6 copy.34
  759.5 8.8 %scatter_fusion.3 = f32[16,128,128]{2,1,0:T(8,128)S(1)} fusion(f32[16,128,128]{2,1,0:T(8,128)S(1)} %broadcast.20, s32[64]{0:T(128)S(1)} %copy-done.6, f32[64,128,128]{2,1,0:T(8,128)} %copy.34), kind=kCustom, calls=%fused_computation.7 | custom fusion | flops 1048576 | bytes 12583168 | tf_op jit(solution)/shard_map/scatter-add | solution.py:17
  769.3 66.3 %all-reduce.5.cloned.1.call-done = f32[2048,128]{1,0:T(8,128)} async-done(((f32[2048,128]{1,0:T(8,128)}), f32[2048,128]{1,0:T(8,128)}) %all-reduce.5.cloned.1.call-update) | async-done | bytes 1048592 | tf_op jit(solution)/shard_map/psum | solution.py:39
  835.6 3.3 multiply_add_fusion
  (37 shorter events, 11.4 us)
Async XLA Ops:
  7.2 4.7 copy-start
  7.2 249.2 %reduce-scatter.3.cloned.1.call-start = ((), (), s32[]{:S(2)}) async-start(), calls=%async_computation.2 | async-start | bytes 2162688 | tf_op jit(solution)/shard_map/reduce_scatter | solution.py:30
  22.6 1.6 copy-start.3
  37.7 218.6 %copy-start.4 = (f32[1,128]{1,0:T(1,128)S(1)}, f32[1,128]{1,0:T(1,128)}, u32[]{:S(2)}) copy-start(f32[1,128]{1,0:T(1,128)} %param.12) | copy-start | bytes 1540
  37.7 218.6 %copy-start.5 = (f32[1,128]{1,0:T(1,128)S(1)}, f32[1,128]{1,0:T(1,128)}, u32[]{:S(2)}) copy-start(f32[1,128]{1,0:T(1,128)} %param.13) | copy-start | bytes 1540
  37.7 296.4 %all-gather.3.cloned.1.call-start = ((), (), s32[]{:S(2)}) async-start(), calls=%async_computation.3 | async-start | bytes 1081344 | tf_op jit(solution)/shard_map/all_gather | solution.py:32
  257.9 165.8 %all-reduce.3.cloned.1.call-start = ((), (), s32[]{:S(2)}) async-start(), calls=%async_computation.4 | async-start | bytes 2097152 | tf_op jit(solution)/shard_map/psum | solution.py:39
  341.9 5.7 copy-start.6
  356.4 1.0 copy-start.2
  357.4 311.3 %reduce-scatter.5.cloned.1.call-start = ((), (), s32[]{:S(2)}) async-start(), calls=%async_computation.5 | async-start | bytes 2162688 | tf_op jit(solution)/shard_map/reduce_scatter | solution.py:30
  453.9 292.1 %all-gather.5.cloned.1.call-start = ((), (), s32[]{:S(2)}) async-start(), calls=%async_computation.6 | async-start | bytes 1081344 | tf_op jit(solution)/shard_map/all_gather | solution.py:32
  670.3 165.3 %all-reduce.5.cloned.1.call-start = ((), (), s32[]{:S(2)}) async-start(), calls=%async_computation.7 | async-start | bytes 2097152 | tf_op jit(solution)/shard_map/psum | solution.py:39
  768.3 1.0 copy-start.1
Sparse Core Ops, SparseCore 0:
  37.9 218.4 reduce-scatter.2
  259.9 74.2 all-gather.2
  357.5 66.1 all-reduce.2
  454.0 214.5 reduce-scatter.4
  671.7 74.3 all-gather.4
  769.4 66.1 all-reduce.4
where the time goes:
time: 847 us; the launch traced here: 846 us
  waiting for transfers between devices  718 us (85%)
  other arithmetic  55.7 us (7%)
  local copies, waits for them, and re-layouts  38.7 us (5%)
  matrix products  19.1 us (2%)
  between operations  14.2 us (2%)
    reduce_scatter x2, waiting for transfers between devices, residual_pass(): lax.psum_scatter(partial_value, 'band', scatter_dimension=0, tiled=True)  433 us
    all_gather x2, waiting for transfers between devices, residual_pass(): lax.all_gather(resid.astype(jnp.bfloat16), 'band', axis=0, tiled=True)  152 us
    psum x2, waiting for transfers between devices, summed_grad(): return lax.psum(part, 'shot')  133 us
    scatter-add x2, other arithmetic, residual_pass(): partial_value = jax.ops.segment_sum(prod, bundle_of, num_segments=bundles)  27 us
    scatter-add x2, other arithmetic, adjoint_part(): jax.ops.segment_sum(contrib, cellblock_of, num_segments=cell_blocks)  17.6 us
  transfers between devices with their start and end apart: 6, of which 6 were waited for; matrix products, arithmetic and copies ran while one was open for 0% of the time, Pallas kernels for 0%

commit v1 on v0

--- a/solution.py
+++ b/solution.py
@@ -29,7 +29,12 @@
         partial_value = jax.ops.segment_sum(prod, bundle_of, num_segments=bundles)
         pred = lax.psum_scatter(partial_value, "band", scatter_dimension=0, tiled=True)
         resid = pick_weight[:, :, None] * (pred - observed[:, :, None])
-        resid_all = lax.all_gather(resid.astype(jnp.bfloat16), "band", axis=0, tiled=True)
+        resid_all = jnp.concatenate(
+            lax.all_to_all(
+                jnp.stack([resid.astype(jnp.bfloat16)] * lax.axis_size("band")), "band", 0, 0
+            ),
+            axis=0,
+        )
         return (resid, adjoint_part(sensitivity, bundle_of, cellblock_of, resid_all, cell_blocks))
 
     probe1 = (state + 0.5 * prior_velocity).astype(jnp.bfloat16)

time: 847 us -> 751 us (0.89)
  waiting for transfers between devices: 718 us -> 586 us
  blocking collectives: 0 us -> 28.7 us
    all_gather x2 -> x0, waiting for transfers between devices: 152 us -> none  [residual_pass(): lax.all_gather(resid.astype(jnp.bfloat16), 'band', axis=0, tiled=True)]
    all_to_all x0 -> x1, blocking collectives: none -> 28.7 us  [residual_pass(): lax.all_to_all(jnp.stack([resid.astype(jnp.bfloat16)] * lax.axis_size('ba...]
    all_to_all x0 -> x1, waiting for transfers between devices: none -> 20.8 us  [residual_pass(): lax.all_to_all(jnp.stack([resid.astype(jnp.bfloat16)] * lax.axis_size('ba...]
  transfers between devices with their start and end apart: 6 -> 5, of which waited for: 6 -> 5; matrix products, arithmetic and copies ran while one was open for 0% -> 0% of each run, Pallas kernels for 0% -> 0%
where the time goes in v1:
time: 751 us; the launch traced here: 749 us
  waiting for transfers between devices  586 us (78%)
  other arithmetic  55.1 us (7%)
  local copies, waits for them, and re-layouts  37.7 us (5%)
  blocking collectives  28.7 us (4%)
  matrix products  19.1 us (3%)
  between operations  13.9 us (2%)
  starting transfers between devices  8.2 us (1%)
    reduce_scatter x2, waiting for transfers between devices, residual_pass(): lax.psum_scatter(partial_value, 'band', scatter_dimension=0, tiled=True)  433 us
    psum x2, waiting for transfers between devices, summed_grad(): return lax.psum(part, 'shot')  133 us
    all_to_all x1, blocking collectives, residual_pass(): lax.all_to_all(jnp.stack([resid.astype(jnp.bfloat16)] * lax.axis_size('ba...  28.7 us
    scatter-add x2, other arithmetic, residual_pass(): partial_value = jax.ops.segment_sum(prod, bundle_of, num_segments=bundles)  27.1 us
    all_to_all x1, waiting for transfers between devices, residual_pass(): lax.all_to_all(jnp.stack([resid.astype(jnp.bfloat16)] * lax.axis_size('ba...  20.8 us
    scatter-add x2, other arithmetic, adjoint_part(): jax.ops.segment_sum(contrib, cellblock_of, num_segments=cell_blocks)  17.6 us
  transfers between devices with their start and end apart: 5, of which 5 were waited for; matrix products, arithmetic and copies ran while one was open for 0% of the time, Pallas kernels for 0%

profile of v1, /device:TPU:2, one launch (start us, length us, event | category | flops | bytes accessed | tf_op | source)
XLA Modules:
  0.0 749.1 jit_solution(2963647071339239053)
XLA Ops:
  9.7 2.2 gather_fusion
  11.9 5.2 convolution_bitcast_fusion.3
  17.0 5.6 copy.22
  24.2 13.5 %scatter_fusion = f32[32,128,128]{2,1,0:T(8,128)} fusion(f32[32,128,128]{2,1,0:T(8,128)} %broadcast.27.clone, s32[64]{0:T(128)S(1)} %copy-done.3, f32[64,128,128]{2,1,0:T(8,128)} %copy.22), kind=kCustom, calls=%fused_computation.4 | custom fusion | flops 1048576 | bytes 12583168 | tf_op jit(solution)/shard_map/scatter-add | solution.py:29
  37.8 218.0 %reduce-scatter.3.cloned.1.call-done = f32[1,128,128]{2,1,0:T(8,128)} async-done(((f32[32,128,128]{2,1,0:T(8,128)}), f32[1,128,128]{2,1,0:T(8,128)}) %reduce-scatter.3.cloned.1.call-update) | async-done | bytes 65552 | tf_op jit(solution)/shard_map/reduce_scatter | solution.py:30
  257.9 8.0 %all-to-all-start = ((bf16[32,1,128,128]{3,2,1,0:T(8,128)(2,1)}), bf16[32,1,128,128]{3,2,1,0:T(8,128)(2,1)S(1)}, u32[]{:S(2)}, u32[]{:S(2)}) async-start(bf16[32,1,128,128]{3,2,1,0:T(8,128)(2,1)} %stack.4), calls=%async_computation.1 | async-start | bytes 2097152 | tf_op jit(solution)/shard_map/all_to_all | solution.py:33
  266.1 20.8 %all-to-all-done = bf16[32,1,128,128]{3,2,1,0:T(8,128)(2,1)S(1)} async-done(((bf16[32,1,128,128]{3,2,1,0:T(8,128)(2,1)}), bf16[32,1,128,128]{3,2,1,0:T(8,128)(2,1)S(1)}, u32[]{:S(2)}, u32[]{:S(2)}) %all-to-all-start) | async-done | bytes 1048608 | tf_op jit(solution)/shard_map/all_to_all | solution.py:33
  286.9 2.1 gather_fusion.1
  289.0 4.4 convolution_bitcast_fusion.2
  293.4 5.6 copy.24
  299.1 8.8 %scatter_fusion.1 = f32[16,128,128]{2,1,0:T(8,128)S(1)} fusion(f32[16,128,128]{2,1,0:T(8,128)S(1)} %broadcast.26.clone, s32[64]{0:T(128)S(1)} %copy-done.6, f32[64,128,128]{2,1,0:T(8,128)} %copy.24), kind=kCustom, calls=%fused_computation.5 | custom fusion | flops 1048576 | bytes 12583168 | tf_op jit(solution)/shard_map/scatter-add | solution.py:17
  309.0 66.4 %all-reduce.3.cloned.1.call-done = f32[2048,128]{1,0:T(8,128)} async-done(((f32[2048,128]{1,0:T(8,128)}), f32[2048,128]{1,0:T(8,128)}) %all-reduce.3.cloned.1.call-update) | async-done | bytes 1048592 | tf_op jit(solution)/shard_map/psum | solution.py:44
  377.5 2.2 gather_fusion.2
  379.7 5.2 convolution_bitcast_fusion.1
  384.9 5.6 copy.26
  392.1 13.5 %scatter_fusion.2 = f32[32,128,128]{2,1,0:T(8,128)} fusion(f32[32,128,128]{2,1,0:T(8,128)} %broadcast.27, s32[64]{0:T(128)S(1)} %copy-done.3, f32[64,128,128]{2,1,0:T(8,128)} %copy.26), kind=kCustom, calls=%fused_computation.6 | custom fusion | flops 1048576 | bytes 12583168 | tf_op jit(solution)/shard_map/scatter-add | solution.py:29
  405.7 214.6 %reduce-scatter.5.cloned.1.call-done = f32[1,128,128]{2,1,0:T(8,128)} async-done(((f32[32,128,128]{2,1,0:T(8,128)}), f32[1,128,128]{2,1,0:T(8,128)}) %reduce-scatter.5.cloned.1.call-update) | async-done | bytes 65552 | tf_op jit(solution)/shard_map/reduce_scatter | solution.py:30
  622.1 28.7 %all_to_all.10 = bf16[32,1,128,128]{3,2,1,0:T(8,128)(2,1)S(1)} all-to-all(bf16[32,1,128,128]{3,2,1,0:T(8,128)(2,1)S(1)} %stack.5), channel_id=1, replica_groups=mesh['shot'=8,'band'=32] {'band'}, dimensions={0} | all-to-all | bytes 2097152 | tf_op jit(solution)/shard_map/all_to_all | solution.py:33
  650.8 2.1 gather_fusion.3
  652.9 4.4 convolution_bitcast_fusion
  657.3 5.6 copy.28
  663.0 8.8 %scatter_fusion.3 = f32[16,128,128]{2,1,0:T(8,128)S(1)} fusion(f32[16,128,128]{2,1,0:T(8,128)S(1)} %broadcast.26, s32[64]{0:T(128)S(1)} %copy-done.6, f32[64,128,128]{2,1,0:T(8,128)} %copy.28), kind=kCustom, calls=%fused_computation.7 | custom fusion | flops 1048576 | bytes 12583168 | tf_op jit(solution)/shard_map/scatter-add | solution.py:17
  672.8 66.5 %all-reduce.5.cloned.1.call-done = f32[2048,128]{1,0:T(8,128)} async-done(((f32[2048,128]{1,0:T(8,128)}), f32[2048,128]{1,0:T(8,128)}) %all-reduce.5.cloned.1.call-update) | async-done | bytes 1048592 | tf_op jit(solution)/shard_map/psum | solution.py:44
  739.3 3.3 multiply_add_fusion
  (36 shorter events, 14.0 us)
Async XLA Ops:
  7.2 4.7 copy-start
  7.2 248.6 %reduce-scatter.3.cloned.1.call-start = ((), (), s32[]{:S(2)}) async-start(), calls=%async_computation.4 | async-start | bytes 2162688 | tf_op jit(solution)/shard_map/reduce_scatter | solution.py:30
  22.6 1.6 copy-start.3
  37.7 218.0 %copy-start.4 = (f32[1,128]{1,0:T(1,128)S(1)}, f32[1,128]{1,0:T(1,128)}, u32[]{:S(2)}) copy-start(f32[1,128]{1,0:T(1,128)} %param.12) | copy-start | bytes 1540
  37.8 218.0 %copy-start.5 = (f32[1,128]{1,0:T(1,128)S(1)}, f32[1,128]{1,0:T(1,128)}, u32[]{:S(2)}) copy-start(f32[1,128]{1,0:T(1,128)} %param.13) | copy-start | bytes 1540
  257.9 29.0 %all-to-all-start = ((bf16[32,1,128,128]{3,2,1,0:T(8,128)(2,1)}), bf16[32,1,128,128]{3,2,1,0:T(8,128)(2,1)S(1)}, u32[]{:S(2)}, u32[]{:S(2)}) async-start(bf16[32,1,128,128]{3,2,1,0:T(8,128)(2,1)} %stack.4), calls=%async_computation.1 | async-start | bytes 2097152 | tf_op jit(solution)/shard_map/all_to_all | solution.py:33
  266.0 109.5 %all-reduce.3.cloned.1.call-start = ((), (), s32[]{:S(2)}) async-start(), calls=%async_computation.5 | async-start | bytes 2097152 | tf_op jit(solution)/shard_map/psum | solution.py:44
  293.4 5.7 copy-start.6
  307.9 1.0 copy-start.2
  308.9 311.3 %reduce-scatter.5.cloned.1.call-start = ((), (), s32[]{:S(2)}) async-start(), calls=%async_computation.6 | async-start | bytes 2162688 | tf_op jit(solution)/shard_map/reduce_scatter | solution.py:30
  405.6 333.6 %all-reduce.5.cloned.1.call-start = ((), (), s32[]{:S(2)}) async-start(), calls=%async_computation.7 | async-start | bytes 2097152 | tf_op jit(solution)/shard_map/psum | solution.py:44
  671.8 1.0 copy-start.1
Sparse Core Ops, SparseCore 0:
  37.9 217.8 reduce-scatter.2
  309.1 66.3 all-reduce.2
  405.7 214.4 reduce-scatter.4
  672.9 66.2 all-reduce.4
